TPU v7x, 32 devices: a whole 2x2x4 slice. The times are simulated.
32 devices in a mesh: stream: 16 (over z, y, core), span: 2 (over x).
Axes of the slice: x: 2, y: 2, z: 4, core: 2. Of those that a mesh axis runs over, the one named last changes fastest.
Arguments:
- basis: float32 [4, 10, 128, 8, 256], P(None, None, 'stream', None, 'span'), may hold values from -6 to 6
- coeffs: float32 [4], replicated, may hold values from -3 to 3
- mixing_matrix: float32 [10, 10], replicated, may hold values from -2 to 2
- base_speed: float32 [128, 8, 256], P('stream', None, 'span'), may hold values from 0.5 to 1.5
- span_speed: float32 [128, 8, 256], P('stream', None, 'span'), may hold values from -2.4 to 2.4
- polymer_gain: float32 [128, 8, 256], P('stream', None, 'span'), may hold values from 0.3 to 3
Outputs:
- proj: float32 [4, 4], replicated
- rfactor: float32 [4, 4], replicated
- basis_new: float32 [4, 10, 128, 8, 256], P(None, None, 'stream', None, 'span')
All inputs are finite; a program needn't handle non-finite values.
Results may differ from a plain program's by a relative error of at most 0.00025.
Values sent between devices are 32-bit elements; how exact they have to be, the bound alone decides.
A program may use at most 64 MiB of HBM per device.

v0:
```python
import functools

import jax
import jax.numpy as jnp
from jax import lax
from jax.experimental import pallas as pl
from jax.experimental.pallas import tpu as pltpu
from jax.sharding import PartitionSpec as P

STEPS = 4
DEEP = 4
WIDE = 2 * DEEP
MESH = pl.DeviceIdType.MESH


def total(terms):
    terms = list(terms)
    while len(terms) > 1:
        pairs = [terms[i] + terms[i + 1] for i in range(0, len(terms) - 1, 2)]
        terms = pairs + terms[len(terms) - len(terms) % 2 :]
    return terms[0]


def span_offsets(span):
    return () if span == 1 else ((1,) if span == 2 else (-1, 1))


def partners(span):
    dzs = span_offsets(span)
    return [(dx, 0) for dx in (-1, 1)] + [(0, dz) for dz in dzs] + [
        (dx, dz) for dx in (-1, 1) for dz in dzs
    ]


def near_and_far(streams):
    near = 16 if streams % 16 == 0 else 1
    return near, streams // near


def krylov_kernel(
    streams, spans,
    coeffs_in, mix_in, basis, base, span_speed, gain,
    krylov_out, sums_out,
    ext, states, held, pack, packs, edge, edges_in, strips, rim_rows, coef, strip_coef, acc, rows, near_rows, far_rows, coeffs, mix,
    in_sem, out_sem, send_sem, recv_sem, plane_send, plane_recv, row_send, row_recv,
):
    m, fields, planes = basis.shape[0], basis.shape[1], basis.shape[2]
    steps = STEPS
    lanes = basis.shape[4]
    sx, sz = lax.axis_index("stream"), lax.axis_index("span")
    near, far = near_and_far(streams)
    near_group = near * spans
    place = lax.rem(sx, near)
    near_index, far_index = place * spans + sz, sx // near

    def near_device(d):
        other = lax.rem(near_index + d, near_group)
        return (sx - place + other // spans, lax.rem(other, spans))

    def far_device(d):
        return (lax.rem(far_index + d, far) * near + place, sz)

    def device(dx, dz):
        return (lax.rem(sx + dx + streams, streams), lax.rem(sz + dz + spans, spans))

    barrier = pltpu.get_barrier_semaphore()

    own = pl.ds(DEEP, planes)
    loads = [
        pltpu.make_async_copy(basis.at[j], held.at[j], in_sem.at[j]) for j in range(m)
    ] + [
        pltpu.make_async_copy(ref, ext.at[fields + i, own], in_sem.at[m + i])
        for i, ref in enumerate((base, span_speed, gain))
    ] + [
        pltpu.make_async_copy(coeffs_in, coeffs, in_sem.at[m + 3]),
        pltpu.make_async_copy(mix_in, mix, in_sem.at[m + 4]),
    ]
    for load in loads:
        load.start()
    slots = partners(spans)
    greeted = [near_device(d) for d in range(1, near_group)]
    greeted += [far_device(d) for d in range(1, far)]
    if far > 1:
        greeted += [device(dx, dz) for dx, dz in slots]
    for other in greeted:
        pl.semaphore_signal(barrier, inc=1, device_id=other, device_id_type=MESH)

    lane = lax.broadcasted_iota(jnp.int32, (8, lanes), 1)
    row = lax.broadcasted_iota(jnp.int32, (8, lanes), 0)

    def packed(field, values):
        out = jnp.zeros((8, lanes), jnp.float32)
        for x in range(planes):
            at = WIDE * (x + DEEP)
            moved = pltpu.roll(values[x], DEEP + at, 1)
            out = jnp.where((lane >= at) & (lane < at + WIDE), moved, out)
        pack[field] = out

    sends, plane_sends = [], []

    def send(src, dst, dx, dz):
        i = len(sends)
        copy = pltpu.make_async_remote_copy(
            src_ref=src, dst_ref=dst, send_sem=send_sem.at[i], recv_sem=recv_sem.at[i],
            device_id=device(dx, dz), device_id_type=MESH,
        )
        copy.start()
        sends.append(copy)
        return copy

    for load in loads[m:]:
        load.wait()
    pl.semaphore_wait(barrier, len(greeted))
    third = pl.ds(fields, 3)
    send(ext.at[third, pl.ds(planes + 1, DEEP - 1)], ext.at[third, pl.ds(1, DEEP - 1)], 1, 0)
    send(ext.at[third, pl.ds(DEEP, DEEP - 1)], ext.at[third, pl.ds(planes + DEEP, DEEP - 1)], -1, 0)
    for i in range(3):
        packed(fields + i, [ext[fields + i, DEEP + x] for x in range(planes)])
    for load in loads[:m]:
        load.wait()
    weights = [coeffs[j] for j in range(m)]

    def start_field(f, carry):
        values = [total(weights[j] * held[j, f, x] for j in range(m)) for x in range(planes)]
        for x in range(planes):
            ext[f, DEEP + x] = values[x]
        packed(f, values)
        return carry

    for f in range(fields):
        start_field(f, 0)

    half = DEEP * WIDE
    per = lanes // half
    tops = planes * WIDE
    for e, begin in enumerate((half, tops)):
        for t in range(edge.shape[1]):
            out = jnp.zeros((8, lanes), jnp.float32)
            for j in range(per):
                f = t * per + j
                if f < fields + 3:
                    moved = pltpu.roll(pack[f], (j * half - begin) % lanes, 1)
                    out = jnp.where((lane >= j * half) & (lane < (j + 1) * half), moved, out)
            edge[e, t] = out
    for i, (dx, dz) in enumerate(slots):
        if dx == 0:
            send(pack, packs.at[i - 2], -dx, -dz)
    corner = [slot for slot in slots if slot[0] != 0]
    for i, (dx, dz) in enumerate(corner):
        send(edge.at[1 if dx == -1 else 0], edges_in.at[i], -dx, -dz)
    main = pl.ds(0, fields)
    for side, (src, dst) in enumerate(((planes, 0), (DEEP, planes + DEEP))):
        copy = pltpu.make_async_remote_copy(
            src_ref=ext.at[main, pl.ds(src, DEEP)], dst_ref=ext.at[main, pl.ds(dst, DEEP)],
            send_sem=plane_send.at[side], recv_sem=plane_recv.at[side],
            device_id=device(1 - 2 * side, 0), device_id_type=MESH,
        )
        copy.start()
        plane_sends.append(copy)

    upper = [(i, j) for i in range(m) for j in range(i, m)]
    krylov_pairs = [(k, l) for k in range(steps) for l in range(k, steps)]
    zero = jnp.zeros((8, lanes), jnp.float32)

    def basis_products(f, sums):
        for x in range(planes):
            b = [held[j, f, x] for j in range(m)]
            sums = [s + b[i] * b[j] for s, (i, j) in zip(sums, upper)]
        return sums

    basis_sums = lax.fori_loop(0, fields, basis_products, [zero] * len(upper))
    first = m * steps + len(krylov_pairs)
    for i, s in enumerate(basis_sums):
        acc[first + i] = s

    for copy in sends:
        copy.wait_recv()

    def cooked(u, w):
        return (
            0.05 - 0.5 * u, 0.05 + 0.5 * u, 0.05 - 0.5 * w, 0.05 + 0.5 * w
        )

    for x in range(1, planes + 2 * DEEP - 1):
        for i, value in enumerate(cooked(ext[fields, x], ext[fields + 1, x])):
            coef[i, x] = value

    inside = (lane >= half) & (lane < half + planes * WIDE)
    left_part = lane % WIDE < DEEP

    def strip_pair(f):
        tile, spot = f // per, f % per

        def whole(dz):
            here = pack[f] if dz == 0 else packs[slots.index((0, dz)) - 2, f]
            before = edges_in[corner.index((-1, dz)), tile]
            after = edges_in[corner.index((1, dz)), tile]
            before = pltpu.roll(before, (-spot * half) % lanes, 1)
            after = pltpu.roll(after, (tops + half - spot * half) % lanes, 1)
            return jnp.where(inside, here, jnp.where(lane < half, before, after))

        mine = whole(0)
        dzs = span_offsets(spans)
        left = whole(dzs[0]) if dzs else mine
        right = left if len(dzs) < 2 else whole(dzs[1])
        return jnp.where(left_part, left, mine), jnp.where(left_part, mine, right)

    for f in range(fields):
        for s, value in enumerate(strip_pair(f)):
            strips[0][f, s] = value
    us, ws, gs = (strip_pair(fields + i) for i in range(3))
    for s in range(2):
        for i, value in enumerate(cooked(us[s], ws[s]) + (gs[s],)):
            strip_coef[i, s] = value

    def walls(v):
        up = jnp.where(row < 7, pltpu.roll(v, 7, 0), 0.0)
        down = jnp.where(row > 0, pltpu.roll(v, 1, 0), 0.0)
        return up + down

    def read(k, f, x):
        return ext[f, x] if k == 0 else states[k - 1][f, x]

    def strip_step(k):
        def field(f, carry):
            weight = [mix[f, g] for g in range(fields)]
            done = []
            for s in range(2):
                mixed = total(a * strips[k][g, s] for g, a in enumerate(weight))
                v = strips[k][f, s]
                done.append(
                    strip_coef[0, s] * pltpu.roll(v, lanes - WIDE, 1)
                    + strip_coef[1, s] * pltpu.roll(v, WIDE, 1)
                    + strip_coef[2, s] * pltpu.roll(v, lanes - 1, 1)
                    + strip_coef[3, s] * pltpu.roll(v, 1, 1)
                    + (0.05 * walls(v) - 0.3 * v)
                    + strip_coef[4, s] * mixed
                )
            for s in range(2):
                strips[k + 1][f, s] = done[s]
            return carry

        for f in range(fields):
            field(f, 0)

    def rims(k):
        def field(f, carry):
            rim_rows[k][f] = jnp.where(
                lane % WIDE == DEEP - 1, strips[k][f, 0],
                pltpu.roll(strips[k][f, 1], lanes - 2, 1),
            )
            return carry

        for f in range(fields):
            field(f, 0)

    def advance(k, which, group):
        if not which:
            return

        def field_group(h, carry):
            some = [group * h + i for i in range(group)]
            weights = [[mix[f, g] for g in range(fields)] for f in some]
            sides = [rim_rows[k][f] for f in some]
            for x in which:
                vs = [read(k, g, x) for g in range(fields)]
                c0, c1, c2, c3 = (coef[i, x] for i in range(4))
                gain_here = ext[fields + 2, x]
                for f, weight, side in zip(some, weights, sides):
                    mixed = total(a * v for a, v in zip(weight, vs))
                    v = read(k, f, x)
                    rim = pltpu.roll(side, (2 * lanes - (WIDE * x + DEEP - 1)) % lanes, 1)
                    ahead = jnp.where(lane == lanes - 1, rim, pltpu.roll(v, lanes - 1, 1))
                    behind = jnp.where(lane == 0, rim, pltpu.roll(v, 1, 1))
                    states[k][f, x] = (
                        (c0 * read(k, f, x + 1) + c1 * read(k, f, x - 1))
                        + (c2 * ahead + c3 * behind)
                        + (0.05 * walls(v) - 0.3 * v)
                        + gain_here * mixed
                    )
            return carry

        for h in range(fields // group):
            field_group(h, 0)

    for k in range(steps):
        rims(k)
        if k < steps - 1:
            strip_step(k)
    large = 5 if fields % 5 == 0 else 1
    last = DEEP + planes
    early = [range(DEEP + 1 + k, last - 1 - k) for k in range(steps)]
    for k in range(steps):
        advance(k, early[k], large)
    for copy in plane_sends:
        copy.wait_recv()
    writes = []
    for k in range(steps):
        needed = range(1 + k, planes + 2 * DEEP - 1 - k)
        advance(k, [x for x in needed if x not in early[k]], large)
        write = pltpu.make_async_copy(states[k].at[:, own], krylov_out.at[k], out_sem.at[k])
        write.start()
        writes.append(write)

    def new_products(f, sums):
        for x in range(planes):
            b = [held[j, f, x] for j in range(m)]
            v = [states[k][f, DEEP + x] for k in range(steps)]
            terms = [b[j] * v[k] for j in range(m) for k in range(steps)]
            terms += [v[k] * v[l] for k, l in krylov_pairs]
            sums = [s + t for s, t in zip(sums, terms)]
        return sums

    new_sums = lax.fori_loop(0, fields, new_products, [zero] * first)
    count = first + len(upper)
    for i, s in enumerate(new_sums):
        rows[pl.ds(i, 1)] = jnp.sum(s, axis=0, keepdims=True)
    for i in range(first, count):
        rows[pl.ds(i, 1)] = jnp.sum(acc[i], axis=0, keepdims=True)
    for i in range(count, rows.shape[0]):
        rows[pl.ds(i, 1)] = jnp.zeros((1, lanes), jnp.float32)
    sums = jnp.sum(rows[...], axis=1, keepdims=True)
    at = lax.broadcasted_iota(jnp.int32, rows.shape, 0)
    spot = lax.broadcasted_iota(jnp.int32, rows.shape, 1)
    local = jnp.sum(jnp.where(at == spot, sums, 0.0), axis=0, keepdims=True)

    def summed(value, gathered, index, size, other, i):
        if size == 1:
            return value
        gathered[index] = value
        for d in range(1, size):
            pltpu.make_async_remote_copy(
                src_ref=gathered.at[index], dst_ref=gathered.at[index],
                send_sem=row_send.at[i], recv_sem=row_recv.at[i],
                device_id=other(d), device_id_type=MESH,
            ).start()
        others = gathered.at[pl.ds(0, size - 1)]
        everyone = pltpu.make_async_remote_copy(
            src_ref=others, dst_ref=others, send_sem=row_send.at[i], recv_sem=row_recv.at[i],
            device_id=other(1), device_id_type=MESH,
        )
        everyone.wait_recv()
        rows_sent.append(everyone)
        return jnp.sum(gathered[...], axis=0)

    rows_sent = []
    close = summed(local, near_rows, near_index, near_group, near_device, 0)
    sums_out[...] = summed(close, far_rows, far_index, far, far_device, 1)
    for copy in rows_sent:
        copy.wait_send()
    for copy in sends + plane_sends:
        copy.wait_send()
    for write in writes:
        write.wait()


def finish_kernel(
    ntot, chunks,
    sums, basis, krylov,
    proj_out, rfactor_out, new_out,
    result, out_sem,
):
    m, fields, planes = basis.shape[0], basis.shape[1], basis.shape[2]
    steps = krylov.shape[0]
    part = fields // chunks

    def piece(c):
        return pl.ds(c * part, part)

    shape = (8, basis.shape[4])
    row = sums[...] * (1.0 / ntot)

    def value(i):
        return jnp.broadcast_to(row[:, i : i + 1], shape)

    p = [[value(steps * j + k) for k in range(steps)] for j in range(m)]
    at = m * steps
    kk, bb = {}, {}
    for k in range(steps):
        for l in range(k, steps):
            kk[k, l] = value(at)
            at += 1
    for i in range(m):
        for j in range(i, m):
            bb[i, j] = bb[j, i] = value(at)
            at += 1
    q = [
        [2.0 * p[i][l] - total(bb[i, j] * p[j][l] for j in range(m)) for l in range(steps)]
        for i in range(m)
    ]
    low, inverse = {}, []
    for l in range(steps):
        for k in range(l, steps):
            g = kk[l, k] - total(p[i][l] * q[i][k] for i in range(m))
            for j in range(l):
                g = g - low[k, j] * low[l, j]
            if k == l:
                low[l, l] = jnp.sqrt(g)
                inverse.append(1.0 / low[l, l])
            else:
                low[k, l] = g * inverse[l]

    x = lax.broadcasted_iota(jnp.int32, shape, 0)
    y = lax.broadcasted_iota(jnp.int32, shape, 1)
    proj = jnp.zeros(shape, jnp.float32)
    for j in range(m):
        for k in range(steps):
            proj = jnp.where((x == j) & (y == k), p[j][k], proj)
    proj_out[...] = proj[:m, :steps]
    factor = jnp.zeros(shape, jnp.float32)
    for k, l in low:
        factor = jnp.where((x == l) & (y == k), low[k, l], factor)
    rfactor_out[...] = factor[:steps, :steps]

    writes = []
    for c in range(chunks):
        def one(i, carry, c=c):
            f = c * part + i
            for half in range(0, planes, 4):
                values = []
                for s in range(half, min(half + 4, planes)):
                    b = [basis[j, f, s] for j in range(m)]
                    done = []
                    for k in range(steps):
                        v = krylov[k, f, s] - total(p[j][k] * b[j] for j in range(m))
                        for l in range(k):
                            v = v - low[k, l] * done[l]
                        done.append(v * inverse[k])
                        values.append((k, s, done[k]))
                for k, s, value in values:
                    result[k, f, s] = value
            return carry

        lax.fori_loop(0, part, one, 0)
        write = pltpu.make_async_copy(
            result.at[:, piece(c)], new_out.at[:, piece(c)], out_sem.at[c]
        )
        write.start()
        writes.append(write)
    for write in writes:
        write.wait()


def on_device(streams, spans, basis, coeffs, mixing_matrix, base_speed, span_speed, polymer_gain):
    m, fields, planes, height, lanes = basis.shape
    n = streams * spans
    near, far = near_and_far(streams)
    f32 = jnp.float32
    deep = planes + 2 * DEEP
    count = m * STEPS + STEPS * (STEPS + 1) // 2 + m * (m + 1) // 2
    padded = -(-count // 8) * 8
    links = 2 + len(partners(spans))
    spans_beside = len(span_offsets(spans))
    corners = 2 + 2 * spans_beside
    tiles = -(-(fields + 3) * DEEP * WIDE // lanes)
    hbm = pl.BlockSpec(memory_space=pltpu.HBM)
    anywhere = pl.BlockSpec(memory_space=pl.ANY)
    vmem = pl.BlockSpec(memory_space=pltpu.VMEM)
    vector = (fields, planes, height, lanes)
    krylov, sums = pl.pallas_call(
        functools.partial(krylov_kernel, streams, spans),
        out_shape=(
            jax.ShapeDtypeStruct((STEPS,) + vector, f32),
            jax.ShapeDtypeStruct((1, lanes), f32),
        ),
        in_specs=[hbm] * 6,
        out_specs=(anywhere, vmem),
        scratch_shapes=[
            pltpu.VMEM((fields + 3, deep, height, lanes), f32),
            [pltpu.VMEM((fields, deep, height, lanes), f32)] * STEPS,
            pltpu.VMEM((m,) + vector, f32),
            pltpu.VMEM((fields + 3, height, lanes), f32),
            pltpu.VMEM((max(spans_beside, 1), fields + 3, height, lanes), f32),
            pltpu.VMEM((2, tiles, height, lanes), f32),
            pltpu.VMEM((corners, tiles, height, lanes), f32),
            [pltpu.VMEM((fields, 2, height, lanes), f32)] * STEPS,
            [pltpu.VMEM((fields, height, lanes), f32)] * STEPS,
            pltpu.VMEM((4, deep, height, lanes), f32),
            pltpu.VMEM((5, 2, height, lanes), f32),
            pltpu.VMEM((count, height, lanes), f32),
            pltpu.VMEM((padded, lanes), f32),
            pltpu.VMEM((near * spans, 1, lanes), f32),
            pltpu.VMEM((far, 1, lanes), f32),
            pltpu.SMEM(coeffs.shape, f32),
            pltpu.SMEM(mixing_matrix.shape, f32),
            pltpu.SemaphoreType.DMA((m + 5,)),
            pltpu.SemaphoreType.DMA((STEPS,)),
            pltpu.SemaphoreType.DMA((links,)),
            pltpu.SemaphoreType.DMA((links,)),
            pltpu.SemaphoreType.DMA((2,)),
            pltpu.SemaphoreType.DMA((2,)),
            pltpu.SemaphoreType.DMA((2,)),
            pltpu.SemaphoreType.DMA((2,)),
        ],
        compiler_params=pltpu.CompilerParams(
            collective_id=0, has_side_effects=True, vmem_limit_bytes=24 * 2**20
        ),
        name="krylov",
    )(*(
        pltpu.with_memory_space_constraint(x, pltpu.HBM)
        for x in (coeffs, mixing_matrix, basis, base_speed, span_speed, polymer_gain)
    ))
    chunks = 5 if fields % 5 == 0 else 1
    return pl.pallas_call(
        functools.partial(finish_kernel, float(m and basis[0].size * n), chunks),
        out_shape=(
            jax.ShapeDtypeStruct((m, STEPS), f32),
            jax.ShapeDtypeStruct((STEPS, STEPS), f32),
            jax.ShapeDtypeStruct((STEPS,) + vector, f32),
        ),
        in_specs=[vmem, vmem, vmem],
        out_specs=(vmem, vmem, hbm),
        scratch_shapes=[
            pltpu.VMEM((STEPS,) + vector, f32),
            pltpu.SemaphoreType.DMA((chunks,)),
        ],
        compiler_params=pltpu.CompilerParams(vmem_limit_bytes=24 * 2**20),
        name="finish",
    )(sums, basis, krylov)


def solution(mesh):
    placed = (
        P(None, None, "stream", None, "span"),
        P(),
        P(),
        P("stream", None, "span"),
        P("stream", None, "span"),
        P("stream", None, "span"),
    )
    return jax.shard_map(
        functools.partial(on_device, mesh.shape["stream"], mesh.shape["span"]),
        mesh=mesh,
        in_specs=placed,
        out_specs=(P(), P(), P(None, None, "stream", None, "span")),
        check_vma=False,
    )
```

profile of v0, /device:TPU:0, one launch (start us, length us, event | category | flops | bytes accessed | tf_op | source)
XLA Modules:
  0.0 23.8 jit_solution(11992541607134276875)
XLA Ops:
  0.6 0.0 copy-start
  0.6 21.1 %krylov.1 = (f32[4,10,8,8,128]{4,3,2,1,0:T(8,128)S(1)}, f32[1,128]{1,0:T(1,128)S(1)}) custom-call(f32[4]{0:T(128)} %coeffs_in.1, f32[10,10]{1,0:T(8,128)} %mix_in.1, f32[4,10,8,8,128]{4,3,2,1,0:T(8,128)} %basis.3, f32[8,8,128]{2,1,0:T(8,128)} %base.1, f32[8,8,128]{2,1,0:T(8,128)} %span_speed.1, f32[8,8,128]{2,1,0:T(8,128)} %gain.1), custom_call_target="tpu_custom_call" | custom-call | tf_op jit(solution)/shard_map/krylov/pallas_call | solution.py:460
  21.7 0.0 copy-done
  21.8 2.1 %finish.1 = (f32[4,4]{1,0:T(4,128)}, f32[4,4]{1,0:T(4,128)}, f32[4,10,8,8,128]{4,3,2,1,0:T(8,128)}) custom-call(f32[1,128]{1,0:T(1,128)S(1)} %get-tuple-element.5.sums, f32[4,10,8,8,128]{4,3,2,1,0:T(8,128)S(1)} %copy-done, f32[4,10,8,8,128]{4,3,2,1,0:T(8,128)S(1)} %get-tuple-element.6.krylov), custom_call_target="tpu_custom_call" | custom-call | tf_op jit(solution)/shard_map/finish/pallas_call | solution.py:504
Async XLA Ops:
  0.6 21.1 %copy-start = (f32[4,10,8,8,128]{4,3,2,1,0:T(8,128)S(1)}, f32[4,10,8,8,128]{4,3,2,1,0:T(8,128)}, u32[]{:S(2)}) copy-start(f32[4,10,8,8,128]{4,3,2,1,0:T(8,128)} %basis.3) | copy-start | bytes 3932164
where the time goes:
time: 24 us; the launch traced here: 23.8 us
  Pallas kernels  23.2 us (97%)
  between operations  0.66 us (3%)
    pallas_call x1, Pallas kernels, on_device(): pl.pallas_call(functools.partial(krylov_kernel, streams, spans), out_shap...  21.1 us
    pallas_call x1, Pallas kernels, on_device(): pl.pallas_call(functools.partial(finish_kernel, float(m and basis[0].size...  2.09 us

commit v1 on v0

--- a/solution.py
+++ b/solution.py
@@ -41,7 +41,7 @@
     streams, spans,
     coeffs_in, mix_in, basis, base, span_speed, gain,
     krylov_out, sums_out,
-    ext, states, held, pack, packs, edge, edges_in, strips, rim_rows, coef, strip_coef, acc, rows, near_rows, far_rows, coeffs, mix,
+    ext, states, held, pack, packs, edge, edges_in, strips, rim_rows, coef, strip_coef, rows, near_rows, far_rows, coeffs, mix,
     in_sem, out_sem, send_sem, recv_sem, plane_send, plane_recv, row_send, row_recv,
 ):
     m, fields, planes = basis.shape[0], basis.shape[1], basis.shape[2]
@@ -53,9 +53,14 @@
     place = lax.rem(sx, near)
     near_index, far_index = place * spans + sz, sx // near
 
+    def turned(value, size):
+        return jnp.where(value >= size, value - size, value)
+
+    near_streams = [sx - place + turned(place + d, near) for d in range(near)]
+    near_spans = [turned(sz + d, spans) for d in range(spans)]
+
     def near_device(d):
-        other = lax.rem(near_index + d, near_group)
-        return (sx - place + other // spans, lax.rem(other, spans))
+        return (near_streams[d // spans], near_spans[d % spans])
 
     def far_device(d):
         return (lax.rem(far_index + d, far) * near + place, sz)
@@ -66,16 +71,19 @@
     barrier = pltpu.get_barrier_semaphore()
 
     own = pl.ds(DEEP, planes)
+    part = fields // 5 if fields % 5 == 0 else fields
+    pieces = [pl.ds(f, part) for f in range(0, fields, part)]
     loads = [
-        pltpu.make_async_copy(basis.at[j], held.at[j], in_sem.at[j]) for j in range(m)
+        pltpu.make_async_copy(basis.at[:, piece], held.at[:, piece], in_sem.at[5 + c])
+        for c, piece in enumerate(pieces)
     ] + [
-        pltpu.make_async_copy(ref, ext.at[fields + i, own], in_sem.at[m + i])
+        pltpu.make_async_copy(ref, ext.at[fields + i, own], in_sem.at[i])
         for i, ref in enumerate((base, span_speed, gain))
     ] + [
-        pltpu.make_async_copy(coeffs_in, coeffs, in_sem.at[m + 3]),
-        pltpu.make_async_copy(mix_in, mix, in_sem.at[m + 4]),
+        pltpu.make_async_copy(coeffs_in, coeffs, in_sem.at[3]),
+        pltpu.make_async_copy(mix_in, mix, in_sem.at[4]),
     ]
-    for load in loads:
+    for load in loads[len(pieces):] + loads[: len(pieces)]:
         load.start()
     slots = partners(spans)
     greeted = [near_device(d) for d in range(1, near_group)]
@@ -108,7 +116,7 @@
         sends.append(copy)
         return copy
 
-    for load in loads[m:]:
+    for load in loads[len(pieces):]:
         load.wait()
     pl.semaphore_wait(barrier, len(greeted))
     third = pl.ds(fields, 3)
@@ -116,8 +124,6 @@
     send(ext.at[third, pl.ds(DEEP, DEEP - 1)], ext.at[third, pl.ds(planes + DEEP, DEEP - 1)], -1, 0)
     for i in range(3):
         packed(fields + i, [ext[fields + i, DEEP + x] for x in range(planes)])
-    for load in loads[:m]:
-        load.wait()
     weights = [coeffs[j] for j in range(m)]
 
     def start_field(f, carry):
@@ -128,6 +134,8 @@
         return carry
 
     for f in range(fields):
+        if f % part == 0:
+            loads[f // part].wait()
         start_field(f, 0)
 
     half = DEEP * WIDE
@@ -170,8 +178,11 @@
 
     basis_sums = lax.fori_loop(0, fields, basis_products, [zero] * len(upper))
     first = m * steps + len(krylov_pairs)
+    count = first + len(upper)
     for i, s in enumerate(basis_sums):
-        acc[first + i] = s
+        rows[pl.ds(first + i, 1)] = jnp.sum(s, axis=0, keepdims=True)
+    for i in range(count, rows.shape[0]):
+        rows[pl.ds(i, 1)] = jnp.zeros((1, lanes), jnp.float32)
 
     for copy in sends:
         copy.wait_recv()
@@ -213,10 +224,11 @@
         for i, value in enumerate(cooked(us[s], ws[s]) + (gs[s],)):
             strip_coef[i, s] = value
 
+    above = jnp.where(row < 7, 0.05, 0.0)
+    below = jnp.where(row > 0, 0.05, 0.0)
+
     def walls(v):
-        up = jnp.where(row < 7, pltpu.roll(v, 7, 0), 0.0)
-        down = jnp.where(row > 0, pltpu.roll(v, 1, 0), 0.0)
-        return up + down
+        return above * pltpu.roll(v, 7, 0) + below * pltpu.roll(v, 1, 0)
 
     def read(k, f, x):
         return ext[f, x] if k == 0 else states[k - 1][f, x]
@@ -233,7 +245,7 @@
                     + strip_coef[1, s] * pltpu.roll(v, WIDE, 1)
                     + strip_coef[2, s] * pltpu.roll(v, lanes - 1, 1)
                     + strip_coef[3, s] * pltpu.roll(v, 1, 1)
-                    + (0.05 * walls(v) - 0.3 * v)
+                    + (walls(v) - 0.3 * v)
                     + strip_coef[4, s] * mixed
                 )
             for s in range(2):
@@ -275,7 +287,7 @@
                     states[k][f, x] = (
                         (c0 * read(k, f, x + 1) + c1 * read(k, f, x - 1))
                         + (c2 * ahead + c3 * behind)
-                        + (0.05 * walls(v) - 0.3 * v)
+                        + (walls(v) - 0.3 * v)
                         + gain_here * mixed
                     )
             return carry
@@ -311,14 +323,11 @@
             sums = [s + t for s, t in zip(sums, terms)]
         return sums
 
-    new_sums = lax.fori_loop(0, fields, new_products, [zero] * first)
-    count = first + len(upper)
+    new_sums = [zero] * first
+    for f in range(fields):
+        new_sums = new_products(f, new_sums)
     for i, s in enumerate(new_sums):
         rows[pl.ds(i, 1)] = jnp.sum(s, axis=0, keepdims=True)
-    for i in range(first, count):
-        rows[pl.ds(i, 1)] = jnp.sum(acc[i], axis=0, keepdims=True)
-    for i in range(count, rows.shape[0]):
-        rows[pl.ds(i, 1)] = jnp.zeros((1, lanes), jnp.float32)
     sums = jnp.sum(rows[...], axis=1, keepdims=True)
     at = lax.broadcasted_iota(jnp.int32, rows.shape, 0)
     spot = lax.broadcasted_iota(jnp.int32, rows.shape, 1)
@@ -431,7 +440,8 @@
                     result[k, f, s] = value
             return carry
 
-        lax.fori_loop(0, part, one, 0)
+        for i in range(part):
+            one(i, 0)
         write = pltpu.make_async_copy(
             result.at[:, piece(c)], new_out.at[:, piece(c)], out_sem.at[c]
         )
@@ -477,13 +487,12 @@
             [pltpu.VMEM((fields, height, lanes), f32)] * STEPS,
             pltpu.VMEM((4, deep, height, lanes), f32),
             pltpu.VMEM((5, 2, height, lanes), f32),
-            pltpu.VMEM((count, height, lanes), f32),
             pltpu.VMEM((padded, lanes), f32),
             pltpu.VMEM((near * spans, 1, lanes), f32),
             pltpu.VMEM((far, 1, lanes), f32),
             pltpu.SMEM(coeffs.shape, f32),
             pltpu.SMEM(mixing_matrix.shape, f32),
-            pltpu.SemaphoreType.DMA((m + 5,)),
+            pltpu.SemaphoreType.DMA((10,)),
             pltpu.SemaphoreType.DMA((STEPS,)),
             pltpu.SemaphoreType.DMA((links,)),
             pltpu.SemaphoreType.DMA((links,)),

time: 24 us -> 24.3 us (1.012)
  Pallas kernels: 23.2 us -> 23.5 us
where the time goes in v1:
time: 24.3 us; the launch traced here: 24.1 us
  Pallas kernels  23.5 us (97%)
  between operations  0.66 us (3%)
    pallas_call x1, Pallas kernels, on_device(): pl.pallas_call(functools.partial(krylov_kernel, streams, spans), out_shap...  21.1 us
    pallas_call x1, Pallas kernels, on_device(): pl.pallas_call(functools.partial(finish_kernel, float(m and basis[0].size...  2.32 us

profile of v1, /device:TPU:0, one launch (start us, length us, event | category | flops | bytes accessed | tf_op | source)
XLA Modules:
  0.0 24.1 jit_solution(7224679371761045257)
XLA Ops:
  0.6 0.0 copy-start
  0.6 21.1 %krylov.1 = (f32[4,10,8,8,128]{4,3,2,1,0:T(8,128)S(1)}, f32[1,128]{1,0:T(1,128)S(1)}) custom-call(f32[4]{0:T(128)} %coeffs_in.1, f32[10,10]{1,0:T(8,128)} %mix_in.1, f32[4,10,8,8,128]{4,3,2,1,0:T(8,128)} %basis.3, f32[8,8,128]{2,1,0:T(8,128)} %base.1, f32[8,8,128]{2,1,0:T(8,128)} %span_speed.1, f32[8,8,128]{2,1,0:T(8,128)} %gain.1), custom_call_target="tpu_custom_call" | custom-call | tf_op jit(solution)/shard_map/krylov/pallas_call | solution.py:470
  21.8 0.0 copy-done
  21.8 2.3 %finish.1 = (f32[4,4]{1,0:T(4,128)}, f32[4,4]{1,0:T(4,128)}, f32[4,10,8,8,128]{4,3,2,1,0:T(8,128)}) custom-call(f32[1,128]{1,0:T(1,128)S(1)} %get-tuple-element.5.sums, f32[4,10,8,8,128]{4,3,2,1,0:T(8,128)S(1)} %copy-done, f32[4,10,8,8,128]{4,3,2,1,0:T(8,128)S(1)} %get-tuple-element.6.krylov), custom_call_target="tpu_custom_call" | custom-call | tf_op jit(solution)/shard_map/finish/pallas_call | solution.py:513
Async XLA Ops:
  0.6 21.2 %copy-start = (f32[4,10,8,8,128]{4,3,2,1,0:T(8,128)S(1)}, f32[4,10,8,8,128]{4,3,2,1,0:T(8,128)}, u32[]{:S(2)}) copy-start(f32[4,10,8,8,128]{4,3,2,1,0:T(8,128)} %basis.3) | copy-start | bytes 3932164

commit v2 on v1

--- a/solution.py
+++ b/solution.py
@@ -157,11 +157,15 @@
     for i, (dx, dz) in enumerate(corner):
         send(edge.at[1 if dx == -1 else 0], edges_in.at[i], -dx, -dz)
     main = pl.ds(0, fields)
-    for side, (src, dst) in enumerate(((planes, 0), (DEEP, planes + DEEP))):
+    mid = DEEP // 2
+    for i, (src, dst, dx) in enumerate((
+        (planes + mid, mid, 1), (DEEP, planes + DEEP, -1),
+        (planes, 0, 1), (DEEP + mid, planes + DEEP + mid, -1),
+    )):
         copy = pltpu.make_async_remote_copy(
-            src_ref=ext.at[main, pl.ds(src, DEEP)], dst_ref=ext.at[main, pl.ds(dst, DEEP)],
-            send_sem=plane_send.at[side], recv_sem=plane_recv.at[side],
-            device_id=device(1 - 2 * side, 0), device_id_type=MESH,
+            src_ref=ext.at[main, pl.ds(src, mid)], dst_ref=ext.at[main, pl.ds(dst, mid)],
+            send_sem=plane_send.at[i], recv_sem=plane_recv.at[i],
+            device_id=device(dx, 0), device_id_type=MESH,
         )
         copy.start()
         plane_sends.append(copy)
@@ -301,15 +305,21 @@
             strip_step(k)
     large = 5 if fields % 5 == 0 else 1
     last = DEEP + planes
-    early = [range(DEEP + 1 + k, last - 1 - k) for k in range(steps)]
+    ready = [range(DEEP + 1 + k, last - 1 - k) for k in range(steps)]
     for k in range(steps):
-        advance(k, early[k], large)
-    for copy in plane_sends:
+        advance(k, ready[k], large)
+    for copy in plane_sends[:2]:
+        copy.wait_recv()
+    for k in range(steps):
+        wider = range(DEEP + 1 + k - mid, last - 1 - k + mid)
+        advance(k, [x for x in wider if x not in ready[k]], large)
+        ready[k] = wider
+    for copy in plane_sends[2:]:
         copy.wait_recv()
     writes = []
     for k in range(steps):
         needed = range(1 + k, planes + 2 * DEEP - 1 - k)
-        advance(k, [x for x in needed if x not in early[k]], large)
+        advance(k, [x for x in needed if x not in ready[k]], large)
         write = pltpu.make_async_copy(states[k].at[:, own], krylov_out.at[k], out_sem.at[k])
         write.start()
         writes.append(write)
@@ -496,8 +506,8 @@
             pltpu.SemaphoreType.DMA((STEPS,)),
             pltpu.SemaphoreType.DMA((links,)),
             pltpu.SemaphoreType.DMA((links,)),
-            pltpu.SemaphoreType.DMA((2,)),
-            pltpu.SemaphoreType.DMA((2,)),
+            pltpu.SemaphoreType.DMA((4,)),
+            pltpu.SemaphoreType.DMA((4,)),
             pltpu.SemaphoreType.DMA((2,)),
             pltpu.SemaphoreType.DMA((2,)),
         ],

time: 24.3 us -> 24.3 us (level)
  no operation moved by 1% of the time
where the time goes in v2:
time: 24.3 us; the launch traced here: 24.1 us
  Pallas kernels  23.5 us (97%)
  between operations  0.66 us (3%)
    pallas_call x1, Pallas kernels, on_device(): pl.pallas_call(functools.partial(krylov_kernel, streams, spans), out_shap...  21.1 us
    pallas_call x1, Pallas kernels, on_device(): pl.pallas_call(functools.partial(finish_kernel, float(m and basis[0].size...  2.32 us

profile of v2, /device:TPU:0, one launch (start us, length us, event | category | flops | bytes accessed | tf_op | source)
XLA Modules:
  0.0 24.1 jit_solution(10391580831084269248)
XLA Ops:
  0.6 0.0 copy-start
  0.6 21.1 %krylov.1 = (f32[4,10,8,8,128]{4,3,2,1,0:T(8,128)S(1)}, f32[1,128]{1,0:T(1,128)S(1)}) custom-call(f32[4]{0:T(128)} %coeffs_in.1, f32[10,10]{1,0:T(8,128)} %mix_in.1, f32[4,10,8,8,128]{4,3,2,1,0:T(8,128)} %basis.3, f32[8,8,128]{2,1,0:T(8,128)} %base.1, f32[8,8,128]{2,1,0:T(8,128)} %span_speed.1, f32[8,8,128]{2,1,0:T(8,128)} %gain.1), custom_call_target="tpu_custom_call" | custom-call | tf_op jit(solution)/shard_map/krylov/pallas_call | solution.py:480
  21.8 0.0 copy-done
  21.8 2.3 %finish.1 = (f32[4,4]{1,0:T(4,128)}, f32[4,4]{1,0:T(4,128)}, f32[4,10,8,8,128]{4,3,2,1,0:T(8,128)}) custom-call(f32[1,128]{1,0:T(1,128)S(1)} %get-tuple-element.5.sums, f32[4,10,8,8,128]{4,3,2,1,0:T(8,128)S(1)} %copy-done, f32[4,10,8,8,128]{4,3,2,1,0:T(8,128)S(1)} %get-tuple-element.6.krylov), custom_call_target="tpu_custom_call" | custom-call | tf_op jit(solution)/shard_map/finish/pallas_call | solution.py:523
Async XLA Ops:
  0.6 21.2 %copy-start = (f32[4,10,8,8,128]{4,3,2,1,0:T(8,128)S(1)}, f32[4,10,8,8,128]{4,3,2,1,0:T(8,128)}, u32[]{:S(2)}) copy-start(f32[4,10,8,8,128]{4,3,2,1,0:T(8,128)} %basis.3) | copy-start | bytes 3932164
